TPU v7x, 32 devices: a whole 2x2x4 slice. The times are simulated.
32 devices in a mesh: seq: 4 (over z), head: 8 (over y, x, core).
Axes of the slice: x: 2, y: 2, z: 4, core: 2. Of those that a mesh axis runs over, the one named last changes fastest.
Arguments:
- queries: bfloat16 [2048, 32, 128], P(('seq', 'head')), may hold values from -6 to 6
- keys: bfloat16 [2048, 32, 128], P(('seq', 'head')), may hold values from -6 to 6
- values: bfloat16 [2048, 32, 128], P(('seq', 'head')), may hold values from -6 to 6
- out_grad: bfloat16 [2048, 32, 128], P(('seq', 'head')), may hold values from -1.5 to 1.5
- level_weights: float32 [32, 12, 2048], P('head', None, 'seq'), may hold values from 0.2 to 2
Outputs:
- query_grad: bfloat16 [2048, 32, 128], P(('seq', 'head'))
- key_grad: bfloat16 [2048, 32, 128], P(('seq', 'head'))
- value_grad: bfloat16 [2048, 32, 128], P(('seq', 'head'))
- weight_grad: float32 [32, 12, 2048], P('head', None, 'seq')
All inputs are finite; a program needn't handle non-finite values.
Results may differ from a plain program's by a relative error of at most 0.0052.
Values may be sent and summed in bfloat16 or wider, within the bound.
A program may use at most 64 MiB of HBM per device.

v0:
```python
import math

import jax
import jax.numpy as jnp
from jax import lax
from jax.sharding import PartitionSpec as P


def partner(value, axis, apart):
    mask = 2**apart
    pairs = [(source, source ^ mask) for source in range(lax.axis_size(axis))]
    return lax.ppermute(value, axis, pairs)


def bit_length(values, number):
    running = jnp.zeros(values.shape, jnp.int32)
    for exponent in range(number):
        running = running + (values >= 2**exponent).astype(jnp.int32)
    return running


def level_factor(degree, head_width):
    base_scale = 1.0 / math.sqrt(head_width)
    if degree == 0:
        return base_scale
    return base_scale * 2.0 ** (-(degree - 1) / 2.0)


def spread_states(lower_source, upper_source):
    far_count = lax.axis_size("seq").bit_length() - 1
    position = lax.axis_index("seq")
    lower_states = []
    upper_states = []
    offset = 1
    running = lower_source
    pending = list(upper_source)
    for degree in range(far_count):
        outgoing = [running] + pending[degree:]
        received = partner(jnp.stack(outgoing), "seq", degree)
        upper_bit = position // 2**degree % 2 == 1
        lower_states.append(jnp.where(upper_bit, received[0], 0.0))
        running = running + received[0]
        upper_states.append(jnp.where(upper_bit, 0.0, received[offset]))
        for later_level in range(degree + 1, far_count):
            pending[later_level] = pending[later_level] + received[offset + later_level - degree]
    return (lower_states, upper_states)


def query_states(query_rows, grad_rows, level_weights, first_far):
    head_width = query_rows.shape[2]
    far_count = level_weights.shape[1] - first_far
    coefficients = jnp.stack(
        [
            level_factor(first_far + degree, head_width) * level_weights[:, first_far + degree, :]
            for degree in range(far_count)
        ]
    )
    scaled = (jnp.transpose(coefficients, (0, 2, 1))[..., None] * grad_rows[None]).astype(
        jnp.bfloat16
    )
    states = jnp.einsum("thd,jthe->jhde", query_rows, scaled, preferred_element_type=jnp.float32)
    return (coefficients, [states[degree] for degree in range(far_count)])


def near_terms(query_rows, key_rows, value_rows, grad_rows, level_weights):
    tok_count = query_rows.shape[0]
    heads_here = query_rows.shape[1]
    head_width = query_rows.shape[2]
    block_rows = min(512, tok_count)
    block_bits = block_rows.bit_length() - 1
    local_bits = tok_count.bit_length() - 1
    pieces = tok_count // block_rows
    zero_block = jnp.zeros((block_rows, heads_here, head_width), jnp.float32)
    zero_weights = jnp.zeros((heads_here, block_rows), jnp.float32)
    query_parts = [zero_block] * pieces
    key_parts = [zero_block] * pieces
    value_parts = [zero_block] * pieces
    weight_rows = [[zero_weights] * pieces for degree in range(local_bits + 1)]
    positions = jnp.arange(block_rows, dtype=jnp.int32)
    crossed = jnp.bitwise_xor(positions[:, None], positions[None, :])
    causal = positions[None, :] <= positions[:, None]
    inside = bit_length(crossed, block_bits)
    scores = jnp.einsum("thd,shd->hts", query_rows, key_rows, preferred_element_type=jnp.float32)
    pulls = jnp.einsum("the,she->hts", grad_rows, value_rows, preferred_element_type=jnp.float32)
    product = jnp.where(causal[None], scores * pulls, 0.0)
    weights = jnp.zeros(scores.shape, jnp.float32)
    for degree in range(block_bits + 1):
        factor = level_factor(degree, head_width)
        matching = (causal & (inside == degree))[None]
        column = (factor * level_weights[:, degree, :])[:, :, None]
        weights = jnp.where(matching, column, weights)
        chosen = jnp.sum(jnp.where(matching, product, 0.0), axis=2)
        weight_rows[degree][0] = factor * chosen
    near_scaled = (weights * scores).astype(jnp.bfloat16)
    near_pulled = (weights * pulls).astype(jnp.bfloat16)
    value_parts[0] = jnp.einsum(
        "hts,the->she", near_scaled, grad_rows, preferred_element_type=jnp.float32
    )
    query_parts[0] = jnp.einsum(
        "hts,shd->thd", near_pulled, key_rows, preferred_element_type=jnp.float32
    )
    key_parts[0] = jnp.einsum(
        "hts,thd->shd", near_pulled, query_rows, preferred_element_type=jnp.float32
    )
    weight_near = [jnp.concatenate(weight_rows[degree], axis=1) for degree in range(local_bits + 1)]
    return (query_parts[0], key_parts[0], value_parts[0], weight_near)


def on_device(queries, keys, values, out_grad, level_weights):
    query_rows, key_rows, value_rows, grad_rows = (
        lax.all_to_all(queries, "head", split_axis=1, concat_axis=0, tiled=True),
        lax.all_to_all(keys, "head", split_axis=1, concat_axis=0, tiled=True),
        lax.all_to_all(values, "head", split_axis=1, concat_axis=0, tiled=True),
        lax.all_to_all(out_grad, "head", split_axis=1, concat_axis=0, tiled=True),
    )
    first_far = query_rows.shape[0].bit_length()
    key_state = jnp.einsum("shd,she->hde", key_rows, value_rows, preferred_element_type=jnp.float32)
    coefficients, upper_parts = query_states(query_rows, grad_rows, level_weights, first_far)
    lower_states, upper_states = spread_states(key_state, upper_parts)
    head_width = query_rows.shape[2]
    far_count = level_weights.shape[1] - first_far
    query_near, key_near, value_near, weight_near = near_terms(
        query_rows, key_rows, value_rows, grad_rows, level_weights
    )
    lower_narrow = jnp.stack([matrix.astype(jnp.bfloat16) for matrix in lower_states])
    far_update = jnp.einsum(
        "the,jhde->jthd", grad_rows, lower_narrow, preferred_element_type=jnp.float32
    )
    query_total = query_near + jnp.sum(
        jnp.transpose(coefficients, (0, 2, 1))[..., None] * far_update, axis=0
    )
    upper_total = upper_states[0]
    for degree in range(1, far_count):
        upper_total = upper_total + upper_states[degree]
    upper_narrow = upper_total.astype(jnp.bfloat16)
    key_total = key_near + jnp.einsum(
        "she,hde->shd", value_rows, upper_narrow, preferred_element_type=jnp.float32
    )
    value_total = value_near + jnp.einsum(
        "shd,hde->she", key_rows, upper_narrow, preferred_element_type=jnp.float32
    )
    factors = jnp.array(
        [level_factor(first_far + degree, head_width) for degree in range(far_count)], jnp.float32
    )
    weight_far = factors[:, None, None] * jnp.sum(query_rows[None] * far_update, axis=-1)
    weight_grad = jnp.stack(
        weight_near + [weight_far[degree].T for degree in range(far_count)], axis=1
    )
    query_out, key_out, value_out = (
        lax.all_to_all(
            query_total.astype(jnp.bfloat16), "head", split_axis=0, concat_axis=1, tiled=True
        ),
        lax.all_to_all(
            key_total.astype(jnp.bfloat16), "head", split_axis=0, concat_axis=1, tiled=True
        ),
        lax.all_to_all(
            value_total.astype(jnp.bfloat16), "head", split_axis=0, concat_axis=1, tiled=True
        ),
    )
    return (query_out, key_out, value_out, weight_grad)


def solution(mesh):
    in_specs = (
        P(("seq", "head"), None, None),
        P(("seq", "head"), None, None),
        P(("seq", "head"), None, None),
        P(("seq", "head"), None, None),
        P("head", None, "seq"),
    )
    out_specs = (
        P(("seq", "head"), None, None),
        P(("seq", "head"), None, None),
        P(("seq", "head"), None, None),
        P("head", None, "seq"),
    )
    return jax.shard_map(
        on_device, mesh=mesh, in_specs=in_specs, out_specs=out_specs, check_vma=False
    )
```

profile of v0, /device:TPU:0, one launch (start us, length us, event | category | flops | bytes accessed | tf_op | source)
XLA Modules:
  0.0 153.6 jit_solution(12001636192345362598)
XLA Ops:
  0.7 2.1 %copy.37 = bf16[64,32,128]{2,0,1:T(8,128)(2,1)} copy(bf16[64,32,128]{2,1,0:T(8,128)(2,1)} %param.6) | data formatting | bytes 1048576 | tf_op args[0]
  2.8 5.2 %all-to-all-start.3 = ((bf16[64,32,128]{2,0,1:T(8,128)(2,1)}), bf16[64,32,128]{2,0,1:T(8,128)(2,1)S(1)}, u32[]{:S(2)}, u32[]{:S(2)}) async-start(bf16[64,32,128]{2,0,1:T(8,128)(2,1)} %copy.37), calls=%async_computation.3 | async-start | bytes 1048576 | tf_op jit(solution)/shard_map/all_to_all | solution.py:111
  8.0 2.0 %copy.27 = bf16[64,32,128]{2,0,1:T(8,128)(2,1)} copy(bf16[64,32,128]{2,1,0:T(8,128)(2,1)} %param.9) | data formatting | bytes 1048576 | tf_op args[3]
  10.0 1.1 fusion.20
  11.1 1.2 fusion.22
  12.3 5.4 %all-to-all-done.3 = bf16[64,32,128]{2,0,1:T(8,128)(2,1)S(1)} async-done(((bf16[64,32,128]{2,0,1:T(8,128)(2,1)}), bf16[64,32,128]{2,0,1:T(8,128)(2,1)S(1)}, u32[]{:S(2)}, u32[]{:S(2)}) %all-to-all-start.3) | async-done | bytes 524320 | tf_op jit(solution)/shard_map/all_to_all | solution.py:111
  17.7 3.5 %all-to-all-start = ((bf16[64,32,128]{2,0,1:T(8,128)(2,1)}), bf16[64,32,128]{2,0,1:T(8,128)(2,1)S(1)}, u32[]{:S(2)}, u32[]{:S(2)}) async-start(bf16[64,32,128]{2,0,1:T(8,128)(2,1)} %copy.27), calls=%async_computation | async-start | bytes 1048576 | tf_op jit(solution)/shard_map/all_to_all | solution.py:114
  21.2 0.8 iota_compare_fusion
  22.0 1.0 copy.31
  23.0 1.2 fusion.24
  24.2 6.7 %all-to-all-done = bf16[64,32,128]{2,0,1:T(8,128)(2,1)S(1)} async-done(((bf16[64,32,128]{2,0,1:T(8,128)(2,1)}), bf16[64,32,128]{2,0,1:T(8,128)(2,1)S(1)}, u32[]{:S(2)}, u32[]{:S(2)}) %all-to-all-start) | async-done | bytes 524320 | tf_op jit(solution)/shard_map/all_to_all | solution.py:114
  30.9 3.5 %all-to-all-start.2 = ((bf16[64,32,128]{2,0,1:T(8,128)(2,1)}), bf16[64,32,128]{2,0,1:T(8,128)(2,1)S(1)}, u32[]{:S(2)}, u32[]{:S(2)}) async-start(bf16[64,32,128]{2,0,1:T(8,128)(2,1)} %copy.31), calls=%async_computation.2 | async-start | bytes 1048576 | tf_op jit(solution)/shard_map/all_to_all | solution.py:112
  34.5 1.0 copy.29
  35.5 1.2 fusion.26
  36.6 1.2 fusion.28
  37.8 6.2 %all-to-all-done.2 = bf16[64,32,128]{2,0,1:T(8,128)(2,1)S(1)} async-done(((bf16[64,32,128]{2,0,1:T(8,128)(2,1)}), bf16[64,32,128]{2,0,1:T(8,128)(2,1)S(1)}, u32[]{:S(2)}, u32[]{:S(2)}) %all-to-all-start.2) | async-done | bytes 524320 | tf_op jit(solution)/shard_map/all_to_all | solution.py:112
  44.1 4.3 %all-to-all-start.1 = ((bf16[64,32,128]{2,0,1:T(8,128)(2,1)}), bf16[64,32,128]{2,0,1:T(8,128)(2,1)}, u32[]{:S(2)}, u32[]{:S(2)}) async-start(bf16[64,32,128]{2,0,1:T(8,128)(2,1)} %copy.29), calls=%async_computation.1 | async-start | bytes 1048576 | tf_op jit(solution)/shard_map/all_to_all | solution.py:113
  48.5 1.3 copy.51
  49.9 1.2 bitcast_convert_fusion.1
  51.0 1.6 %copy.36 = f32[512,4,128]{0,2,1:T(8,128)S(1)} copy(f32[512,4,128]{2,0,1:T(8,128)} %bitcast_convert_fusion.1) | data formatting | bytes 2097152 | tf_op jit(solution)/shard_map/convert_element_type | solution.py:58
  52.6 5.3 %all-to-all-done.1 = bf16[64,32,128]{2,0,1:T(8,128)(2,1)} async-done(((bf16[64,32,128]{2,0,1:T(8,128)(2,1)}), bf16[64,32,128]{2,0,1:T(8,128)(2,1)}, u32[]{:S(2)}, u32[]{:S(2)}) %all-to-all-start.1) | async-done | bytes 524320 | tf_op jit(solution)/shard_map/all_to_all | solution.py:113
  58.0 1.1 copy.30
  60.0 1.6 %collective-permute-start = (f32[3,4,128,128]{3,2,1,0:T(8,128)S(1)}, f32[3,4,128,128]{3,2,1,0:T(8,128)S(1)}, u32[]{:S(2)}, u32[]{:S(2)}) collective-permute-start(f32[3,4,128,128]{3,2,1,0:T(8,128)S(1)} %pad_maximum_fusion), channel_id=1, source_target_pairs={{0,8},{8,0},{16,24},{24,16},{1,9},{9,1},{17,25},{25,17},{2,10},{10... | collective-permute-start | bytes 2359304 | tf_op jit(solution)/shard_map/ppermute | solution.py:12
  61.7 5.9 %multiply_convert_fusion.1 = (bf16[4,512,512]{1,2,0:T(8,128)(2,1)S(1)}, f32[4,512,512]{1,2,0:T(8,128)S(1)}) fusion(f32[4,512]{1,0:T(4,128)S(1)} %get-tuple-element.17, f32[4,512]{1,0:T(4,128)S(1)} %get-tuple-element.18, f32[4,512]{1,0:T(4,128)S(1)} %get-tuple-element.19, f32[4,512]{1,0:T(4,128)S(1)} %get-tuple-element.20, ...), kind=kOutput, calls=%fused_computation.12 | convolution fusion | flops 281018368 | bytes 10043392 | tf_op jit(solution)/shard_map/the,she->hts/dot_general | solution.py:84
  67.8 6.9 %select_reduce_fusion = (f32[4,512]{1,0:T(4,128)S(1)}, f32[4,512]{1,0:T(4,128)S(1)}, f32[4,512]{1,0:T(4,128)S(1)}, f32[4,512]{1,0:T(4,128)S(1)}, f32[4,512]{1,0:...) fusion(pred[512,512]{0,1:T(8,128)(4,1)S(1)} %copy-done.19, ...), kind=kOutput, calls=%fused_computation | convolution fusion | flops 291483648 | bytes 12402688 | tf_op jit(solution)/shard_map/thd,shd->hts/dot_general | solution.py:83
  74.8 0.6 copy-done.21
  75.5 5.2 %fusion.3 = f32[512,4,128]{2,0,1:T(8,128)} fusion(bf16[512,4,128]{2,0,1:T(8,128)(2,1)S(1)} %bitcast.164, f32[4,512,512]{1,2,0:T(8,128)S(1)} %get-tuple-element.34, f32[4,512]{1,0:T(4,128)S(1)} %get-tuple-element.17, f32[4,512]{1,0:T(4,128)S(1)} %get-tuple-element.18, f32[4,512]{1,0:T(4,128)S(1)} %get-tuple-element.19, f32[4,512]{1,0:T(4,128)S(1)} %get-tuple-element.20, ...), kind=kOutput, calls=%fused_computation.22 | convolution fusion | flops 281018368 | bytes 8470528 | tf_op jit(solution)/shard_map/hts,the->she/dot_general | solution.py:96
  80.8 2.7 %collective-permute-start.1 = (f32[2,4,128,128]{3,2,1,0:T(8,128)S(1)}, f32[2,4,128,128]{3,2,1,0:T(8,128)S(1)}, u32[]{:S(2)}, u32[]{:S(2)}) collective-permute-start(f32[2,4,128,128]{3,2,1,0:T(8,128)S(1)} %pad_maximum_fusion.1), channel_id=1, source_target_pairs={{0,16},{8,24},{16,0},{24,8},{1,17},{9,25},{17,1},{25,9},{2,18},{10... | collective-permute-start | bytes 1572872 | tf_op jit(solution)/shard_map/ppermute | solution.py:12
  83.5 1.7 %convolution_bitcast_fusion = f32[512,4,128]{2,0,1:T(8,128)} fusion(bf16[4,512,512]{1,2,0:T(8,128)(2,1)S(1)} %get-tuple-element.30, bf16[512,4,128]{2,0,1:T(8,128)(2,1)S(1)} %bitcast.155), kind=kOutput, calls=%fused_computation.20 | convolution fusion | flops 268435456 | bytes 3670016 | tf_op jit(solution)/shard_map/hts,thd->shd/dot_general | solution.py:102
  85.2 18.7 %collective-permute-done.1 = f32[2,4,128,128]{3,2,1,0:T(8,128)S(1)} collective-permute-done((f32[2,4,128,128]{3,2,1,0:T(8,128)S(1)}, f32[2,4,128,128]{3,2,1,0:T(8,128)S(1)}, u32[]{:S(2)}, u32[]{:S(2)}) %collective-permute-start.1) | collective-permute-done | bytes 524320 | tf_op jit(solution)/shard_map/ppermute | solution.py:12
  103.9 0.8 copy-done.9
  104.8 1.5 fusion.1
  106.3 2.6 %copy.41 = f32[512,4,128]{2,0,1:T(8,128)} copy(f32[512,4,128]{0,2,1:T(8,128)} %get-tuple-element.15) | data formatting | bytes 2097152 | tf_op jit(solution)/shard_map/reduce_sum | solution.py:129
  108.9 2.1 %fusion.7 = bf16[512,4,128]{2,0,1:T(8,128)(2,1)S(1)} fusion(f32[512,4,128]{2,0,1:T(8,128)} %copy.41, bf16[4,512,512]{1,2,0:T(8,128)(2,1)S(1)} %get-tuple-element.30, bf16[512,4,128]{2,0,1:T(8,128)(2,1)S(1)} %bitcast.158), kind=kOutput, calls=%fused_computation.28 | convolution fusion | flops 268959744 | bytes 4194304 | tf_op jit(solution)/shard_map/hts,shd->thd/dot_general | solution.py:99
  110.9 1.2 copy.42
  112.1 4.4 %all-to-all-start.4 = ((bf16[512,4,128]{2,1,0:T(4,128)(2,1)}), bf16[512,4,128]{2,1,0:T(4,128)(2,1)S(1)}, u32[]{:S(2)}, u32[]{:S(2)}) async-start(bf16[512,4,128]{2,1,0:T(4,128)(2,1)} %copy.42), calls=%async_computation.4 | async-start | bytes 1048576 | tf_op jit(solution)/shard_map/all_to_all | solution.py:150
  116.6 1.1 fusion.36
  117.7 1.5 fusion.8
  119.2 1.2 copy.45
  120.4 5.9 %all-to-all-done.4 = bf16[512,4,128]{2,1,0:T(4,128)(2,1)S(1)} async-done(((bf16[512,4,128]{2,1,0:T(4,128)(2,1)}), bf16[512,4,128]{2,1,0:T(4,128)(2,1)S(1)}, u32[]{:S(2)}, u32[]{:S(2)}) %all-to-all-start.4) | async-done | bytes 524320 | tf_op jit(solution)/shard_map/all_to_all | solution.py:150
  126.3 3.5 %all-to-all-start.5 = ((bf16[512,4,128]{2,1,0:T(4,128)(2,1)}), bf16[512,4,128]{2,1,0:T(4,128)(2,1)S(1)}, u32[]{:S(2)}, u32[]{:S(2)}) async-start(bf16[512,4,128]{2,1,0:T(4,128)(2,1)} %copy.45), calls=%async_computation.5 | async-start | bytes 1048576 | tf_op jit(solution)/shard_map/all_to_all | solution.py:153
  130.1 1.2 copy.49
  131.4 8.1 %all-to-all-done.5 = bf16[512,4,128]{2,1,0:T(4,128)(2,1)S(1)} async-done(((bf16[512,4,128]{2,1,0:T(4,128)(2,1)}), bf16[512,4,128]{2,1,0:T(4,128)(2,1)S(1)}, u32[]{:S(2)}, u32[]{:S(2)}) %all-to-all-start.5) | async-done | bytes 524320 | tf_op jit(solution)/shard_map/all_to_all | solution.py:153
  139.5 3.5 %all-to-all-start.6 = ((bf16[512,4,128]{2,1,0:T(4,128)(2,1)}), bf16[512,4,128]{2,1,0:T(4,128)(2,1)S(1)}, u32[]{:S(2)}, u32[]{:S(2)}) async-start(bf16[512,4,128]{2,1,0:T(4,128)(2,1)} %copy.49), calls=%async_computation.6 | async-start | bytes 1048576 | tf_op jit(solution)/shard_map/all_to_all | solution.py:156
  144.2 1.0 copy.43
  145.2 1.0 copy.46
  146.2 6.5 %all-to-all-done.6 = bf16[512,4,128]{2,1,0:T(4,128)(2,1)S(1)} async-done(((bf16[512,4,128]{2,1,0:T(4,128)(2,1)}), bf16[512,4,128]{2,1,0:T(4,128)(2,1)S(1)}, u32[]{:S(2)}, u32[]{:S(2)}) %all-to-all-start.6) | async-done | bytes 524320 | tf_op jit(solution)/shard_map/all_to_all | solution.py:156
  152.7 1.0 copy.50
  (75 shorter events, 3.1 us)
Async XLA Ops:
  0.6 21.4 %copy-start.7 = (bf16[64,32,128]{2,1,0:T(8,128)(2,1)S(1)}, bf16[64,32,128]{2,1,0:T(8,128)(2,1)}, u32[]{:S(2)}) copy-start(bf16[64,32,128]{2,1,0:T(8,128)(2,1)} %param.7) | copy-start | bytes 1572868
  0.6 23.5 %copy-start.20 = (f32[4,12,512]{2,0,1:T(4,128)S(1)}, f32[4,12,512]{2,0,1:T(4,128)}, u32[]{:S(2)}) copy-start(f32[4,12,512]{2,0,1:T(4,128)} %param.10) | copy-start | bytes 294916
  0.7 33.8 %copy-start.8 = (bf16[64,32,128]{2,1,0:T(8,128)(2,1)S(1)}, bf16[64,32,128]{2,1,0:T(8,128)(2,1)}, u32[]{:S(2)}) copy-start(bf16[64,32,128]{2,1,0:T(8,128)(2,1)} %param.8) | copy-start | bytes 1572868
  2.8 14.9 %all-to-all-start.3 = ((bf16[64,32,128]{2,0,1:T(8,128)(2,1)}), bf16[64,32,128]{2,0,1:T(8,128)(2,1)S(1)}, u32[]{:S(2)}, u32[]{:S(2)}) async-start(bf16[64,32,128]{2,0,1:T(8,128)(2,1)} %copy.37), calls=%async_computation.3 | async-start | bytes 1048576 | tf_op jit(solution)/shard_map/all_to_all | solution.py:111
  17.7 13.2 %all-to-all-start = ((bf16[64,32,128]{2,0,1:T(8,128)(2,1)}), bf16[64,32,128]{2,0,1:T(8,128)(2,1)S(1)}, u32[]{:S(2)}, u32[]{:S(2)}) async-start(bf16[64,32,128]{2,0,1:T(8,128)(2,1)} %copy.27), calls=%async_computation | async-start | bytes 1048576 | tf_op jit(solution)/shard_map/all_to_all | solution.py:114
  30.9 13.2 %all-to-all-start.2 = ((bf16[64,32,128]{2,0,1:T(8,128)(2,1)}), bf16[64,32,128]{2,0,1:T(8,128)(2,1)S(1)}, u32[]{:S(2)}, u32[]{:S(2)}) async-start(bf16[64,32,128]{2,0,1:T(8,128)(2,1)} %copy.31), calls=%async_computation.2 | async-start | bytes 1048576 | tf_op jit(solution)/shard_map/all_to_all | solution.py:112
  44.1 13.9 %all-to-all-start.1 = ((bf16[64,32,128]{2,0,1:T(8,128)(2,1)}), bf16[64,32,128]{2,0,1:T(8,128)(2,1)}, u32[]{:S(2)}, u32[]{:S(2)}) async-start(bf16[64,32,128]{2,0,1:T(8,128)(2,1)} %copy.29), calls=%async_computation.1 | async-start | bytes 1048576 | tf_op jit(solution)/shard_map/all_to_all | solution.py:113
  49.9 10.1 %copy-start.2 = (bf16[64,8,4,128]{3,0,1,2:T(8,128)(2,1)}, bf16[64,8,4,128]{3,0,1,2:T(8,128)(2,1)S(1)}, u32[]{:S(2)}) copy-start(bf16[64,8,4,128]{3,0,1,2:T(8,128)(2,1)S(1)} %copy.28) | copy-start | bytes 1572868
  59.1 8.6 %copy-start = (bf16[64,8,4,128]{3,0,1,2:T(8,128)(2,1)}, bf16[64,8,4,128]{3,0,1,2:T(8,128)(2,1)S(1)}, u32[]{:S(2)}) copy-start(bf16[64,8,4,128]{3,0,1,2:T(8,128)(2,1)S(1)} %copy.30) | copy-start | bytes 1572868
  60.0 20.7 %collective-permute-start = (f32[3,4,128,128]{3,2,1,0:T(8,128)S(1)}, f32[3,4,128,128]{3,2,1,0:T(8,128)S(1)}, u32[]{:S(2)}, u32[]{:S(2)}) collective-permute-start(f32[3,4,128,128]{3,2,1,0:T(8,128)S(1)} %pad_maximum_fusion), channel_id=1, source_target_pairs={{0,8},{8,0},{16,24},{24,16},{1,9},{9,1},{17,25},{25,17},{2,10},{10... | collective-permute-start | bytes 2359304 | tf_op jit(solution)/shard_map/ppermute | solution.py:12
  61.6 6.0 %copy-start.10 = (pred[512,512]{0,1:T(8,128)(4,1)S(1)}, pred[512,512]{0,1:T(8,128)(4,1)}, u32[]{:S(2)}) copy-start(pred[512,512]{0,1:T(8,128)(4,1)} %get-tuple-element.36) | copy-start | bytes 786436
  61.6 6.0 %copy-start.11 = (pred[512,512]{0,1:T(8,128)(4,1)S(1)}, pred[512,512]{0,1:T(8,128)(4,1)}, u32[]{:S(2)}) copy-start(pred[512,512]{0,1:T(8,128)(4,1)} %get-tuple-element.37) | copy-start | bytes 786436
  61.6 6.0 %copy-start.12 = (pred[512,512]{0,1:T(8,128)(4,1)S(1)}, pred[512,512]{0,1:T(8,128)(4,1)}, u32[]{:S(2)}) copy-start(pred[512,512]{0,1:T(8,128)(4,1)} %get-tuple-element.38) | copy-start | bytes 786436
  61.6 6.0 %copy-start.13 = (pred[512,512]{0,1:T(8,128)(4,1)S(1)}, pred[512,512]{0,1:T(8,128)(4,1)}, u32[]{:S(2)}) copy-start(pred[512,512]{0,1:T(8,128)(4,1)} %get-tuple-element.39) | copy-start | bytes 786436
  61.7 6.0 %copy-start.14 = (pred[512,512]{0,1:T(8,128)(4,1)S(1)}, pred[512,512]{0,1:T(8,128)(4,1)}, u32[]{:S(2)}) copy-start(pred[512,512]{0,1:T(8,128)(4,1)} %get-tuple-element.40) | copy-start | bytes 786436
  61.7 6.0 %copy-start.15 = (pred[512,512]{0,1:T(8,128)(4,1)S(1)}, pred[512,512]{0,1:T(8,128)(4,1)}, u32[]{:S(2)}) copy-start(pred[512,512]{0,1:T(8,128)(4,1)} %iota_compare_fusion) | copy-start | bytes 786436
  61.7 6.0 %copy-start.16 = (pred[512,512]{0,1:T(8,128)(4,1)S(1)}, pred[512,512]{0,1:T(8,128)(4,1)}, u32[]{:S(2)}) copy-start(pred[512,512]{0,1:T(8,128)(4,1)} %get-tuple-element.41) | copy-start | bytes 786436
  61.7 6.0 %copy-start.17 = (pred[512,512]{0,1:T(8,128)(4,1)S(1)}, pred[512,512]{0,1:T(8,128)(4,1)}, u32[]{:S(2)}) copy-start(pred[512,512]{0,1:T(8,128)(4,1)} %get-tuple-element.42) | copy-start | bytes 786436
  61.7 6.0 %copy-start.18 = (pred[512,512]{0,1:T(8,128)(4,1)S(1)}, pred[512,512]{0,1:T(8,128)(4,1)}, u32[]{:S(2)}) copy-start(pred[512,512]{0,1:T(8,128)(4,1)} %get-tuple-element.43) | copy-start | bytes 786436
  61.7 6.0 %copy-start.19 = (pred[512,512]{0,1:T(8,128)(4,1)S(1)}, pred[512,512]{0,1:T(8,128)(4,1)}, u32[]{:S(2)}) copy-start(pred[512,512]{0,1:T(8,128)(4,1)} %get-tuple-element.44) | copy-start | bytes 786436
  67.7 7.7 %copy-start.3 = (bf16[64,8,4,128]{3,0,1,2:T(8,128)(2,1)S(1)}, bf16[64,8,4,128]{3,0,1,2:T(8,128)(2,1)}, u32[]{:S(2)}) copy-start(bf16[64,8,4,128]{3,0,1,2:T(8,128)(2,1)} %copy-done.2) | copy-start | bytes 1572868
  74.8 0.6 copy-start.21
  80.7 24.1 %copy-start.4 = (f32[512,4,128]{0,2,1:T(8,128)S(1)}, f32[512,4,128]{0,2,1:T(8,128)}, u32[]{:S(2)}) copy-start(f32[512,4,128]{0,2,1:T(8,128)} %copy.51) | copy-start | bytes 3145732
  80.7 25.6 %copy-start.5 = (f32[3,4,128,128]{3,2,1,0:T(8,128)}, f32[3,4,128,128]{3,2,1,0:T(8,128)S(1)}, u32[]{:S(2)}) copy-start(f32[3,4,128,128]{3,2,1,0:T(8,128)S(1)} %collective-permute-done) | copy-start | bytes 2359300
  80.8 23.1 %collective-permute-start.1 = (f32[2,4,128,128]{3,2,1,0:T(8,128)S(1)}, f32[2,4,128,128]{3,2,1,0:T(8,128)S(1)}, u32[]{:S(2)}, u32[]{:S(2)}) collective-permute-start(f32[2,4,128,128]{3,2,1,0:T(8,128)S(1)} %pad_maximum_fusion.1), channel_id=1, source_target_pairs={{0,16},{8,24},{16,0},{24,8},{1,17},{9,25},{17,1},{25,9},{2,18},{10... | collective-permute-start | bytes 1572872 | tf_op jit(solution)/shard_map/ppermute | solution.py:12
  103.9 0.8 copy-start.9
  106.3 11.4 %copy-start.1 = (bf16[64,8,4,128]{3,0,1,2:T(8,128)(2,1)S(1)}, bf16[64,8,4,128]{3,0,1,2:T(8,128)(2,1)}, u32[]{:S(2)}) copy-start(bf16[64,8,4,128]{3,0,1,2:T(8,128)(2,1)} %copy-done) | copy-start | bytes 1572868
  110.9 18.9 %copy-start.6 = (f32[512,4,128]{2,0,1:T(8,128)S(1)}, f32[512,4,128]{2,0,1:T(8,128)}, u32[]{:S(2)}) copy-start(f32[512,4,128]{2,0,1:T(8,128)} %fusion.3) | copy-start | bytes 3145732
  112.1 14.2 %all-to-all-start.4 = ((bf16[512,4,128]{2,1,0:T(4,128)(2,1)}), bf16[512,4,128]{2,1,0:T(4,128)(2,1)S(1)}, u32[]{:S(2)}, u32[]{:S(2)}) async-start(bf16[512,4,128]{2,1,0:T(4,128)(2,1)} %copy.42), calls=%async_computation.4 | async-start | bytes 1048576 | tf_op jit(solution)/shard_map/all_to_all | solution.py:150
  116.6 14.8 %copy-start.22 = (f32[2]{0:T(128)S(1)}, f32[2]{0:T(128)}, u32[]{:S(2)}) copy-start(f32[2]{0:T(128)} %constant.96.clone) | copy-start | bytes 28
  126.3 13.2 %all-to-all-start.5 = ((bf16[512,4,128]{2,1,0:T(4,128)(2,1)}), bf16[512,4,128]{2,1,0:T(4,128)(2,1)S(1)}, u32[]{:S(2)}, u32[]{:S(2)}) async-start(bf16[512,4,128]{2,1,0:T(4,128)(2,1)} %copy.45), calls=%async_computation.5 | async-start | bytes 1048576 | tf_op jit(solution)/shard_map/all_to_all | solution.py:153
  139.5 13.2 %all-to-all-start.6 = ((bf16[512,4,128]{2,1,0:T(4,128)(2,1)}), bf16[512,4,128]{2,1,0:T(4,128)(2,1)S(1)}, u32[]{:S(2)}, u32[]{:S(2)}) async-start(bf16[512,4,128]{2,1,0:T(4,128)(2,1)} %copy.49), calls=%async_computation.6 | async-start | bytes 1048576 | tf_op jit(solution)/shard_map/all_to_all | solution.py:156
where the time goes:
time: 155 us; the launch traced here: 154 us
  waiting for transfers between devices  62.9 us (41%)
  starting transfers between devices  32.2 us (21%)
  matrix products  25.9 us (17%)
  local copies, waits for them, and re-layouts  22.1 us (14%)
  other arithmetic  9.34 us (6%)
    ppermute x2, waiting for transfers between devices, partner(): return lax.ppermute(value, axis, pairs)  18.8 us
    unnamed x51, local copies, waits for them, and re-layouts  8.29 us
    all_to_all x1, waiting for transfers between devices, on_device(): lax.all_to_all(key_total.astype(jnp.bfloat16), 'head', split_axis=0, conc...  8.1 us
    dot_general x1, matrix products, near_terms(): jnp.einsum('thd,shd->hts', query_rows, key_rows, preferred_element_type=j...  6.93 us
    all_to_all x1, waiting for transfers between devices, on_device(): lax.all_to_all(out_grad, 'head', split_axis=1, concat_axis=0, tiled=True)  6.68 us
    all_to_all x1, waiting for transfers between devices, on_device(): lax.all_to_all(value_total.astype(jnp.bfloat16), 'head', split_axis=0, co...  6.5 us
    all_to_all x1, waiting for transfers between devices, on_device(): lax.all_to_all(keys, 'head', split_axis=1, concat_axis=0, tiled=True)  6.23 us
    all_to_all x1, waiting for transfers between devices, on_device(): lax.all_to_all(query_total.astype(jnp.bfloat16), 'head', split_axis=0, co...  5.92 us
  transfers between devices with their start and end apart: 9, of which 8 were waited for; matrix products, arithmetic and copies ran while one was open for 28% of the time, Pallas kernels for 0%

commit v1 on v0

v1 whole, which is shorter than its diff:
```python
import functools
import math

import jax
import jax.numpy as jnp
from jax import lax
from jax.experimental import pallas as pl
from jax.experimental.pallas import tpu as pltpu
from jax.sharding import PartitionSpec as P

MESH = pl.DeviceIdType.MESH
TILE = 128
SIDE = 256
F32 = jnp.float32
BF16 = jnp.bfloat16


def level_factor(degree, head_width):
    base_scale = 1.0 / math.sqrt(head_width)
    if degree == 0:
        return base_scale
    return base_scale * 2.0 ** (-(degree - 1) / 2.0)


def dot(left, right):
    return jnp.dot(left, right, preferred_element_type=F32)


def dot_nt(left, right):
    return lax.dot_general(left, right, (((1,), (1,)), ((), ())), preferred_element_type=F32)


def kernel(
    peers,
    blocks,
    q_ref,
    k_ref,
    v_ref,
    g_ref,
    lw_ref,
    qo_ref,
    ko_ref,
    vo_ref,
    wg_ref,
    stage,
    send_buf,
    rows,
    out_rows,
    land,
    state_out,
    state_in,
    score_t,
    pull_t,
    scaled_t,
    pulled_t,
    level_ref,
    acc,
    acc_t,
    turned,
    send_sem,
    recv_sem,
    out_send_sem,
    out_recv_sem,
    state_send_sem,
    state_recv_sem,
):
    part, heads, width = q_ref.shape
    here = heads // peers
    toks = part * peers
    local_bits = toks.bit_length() - 1
    first_far = local_bits + 1
    far = blocks.bit_length() - 1
    tiles = toks // TILE
    tile_bits = TILE.bit_length() - 1
    sides = toks // SIDE
    me = lax.axis_index("head")
    block = lax.axis_index("seq")

    def peer(offset):
        return lax.rem(me + offset, peers)

    def source(offset):
        return lax.rem(me + peers - offset, peers)

    def block_to(offset):
        return lax.rem(block + offset, blocks)

    def block_from(offset):
        return lax.rem(block + blocks - offset, blocks)

    def part_of(index):
        return pl.ds(pl.multiple_of(index * part, part), part)

    def degree_of(one, other):
        degree = 0
        for shift in range(1, far):
            apart = lax.div(one, 2**shift) != lax.div(other, 2**shift)
            degree = degree + jnp.where(apart, 1, 0)
        return degree

    barrier = pltpu.get_barrier_semaphore()
    for offset in range(1, peers):
        pl.semaphore_signal(barrier, inc=1, device_id=(block, peer(offset)), device_id_type=MESH)
    for offset in range(1, blocks):
        pl.semaphore_signal(barrier, inc=1, device_id=(block_to(offset), me), device_id_type=MESH)

    chunk = 8
    for index, ref in enumerate((q_ref, k_ref, v_ref, g_ref)):
        for start in range(0, part, chunk):
            stage[index, pl.ds(start * heads, chunk * heads), :] = (
                ref[pl.ds(start, chunk)].astype(F32).reshape(chunk * heads, width)
            )

    pl.semaphore_wait(barrier, peers + blocks - 2)

    def input_copy(head, offset):
        return pltpu.make_async_remote_copy(
            src_ref=send_buf.at[head, offset],
            dst_ref=rows.at[head, :, part_of(me), :],
            send_sem=send_sem.at[head, offset],
            recv_sem=recv_sem.at[head, offset],
            device_id=(block, peer(offset)),
            device_id_type=MESH,
        )

    def output_copy(head, offset):
        return pltpu.make_async_remote_copy(
            src_ref=out_rows.at[head, :, part_of(peer(offset)), :],
            dst_ref=land.at[head, offset],
            send_sem=out_send_sem.at[head, offset],
            recv_sem=out_recv_sem.at[head, offset],
            device_id=(block, peer(offset)),
            device_id_type=MESH,
        )

    def state_copy(head, offset):
        other = block_to(offset)
        picked = jnp.where(other > block, 0, 1 + degree_of(block, other))
        return pltpu.make_async_remote_copy(
            src_ref=state_out.at[head, picked],
            dst_ref=state_in.at[head, offset],
            send_sem=state_send_sem.at[head, offset],
            recv_sem=state_recv_sem.at[head, offset],
            device_id=(other, me),
            device_id_type=MESH,
        )

    def send_inputs(head, carry):
        for offset in list(range(1, peers)) + [0]:
            number = peer(offset) * here + head
            for index in range(4):
                picked = stage[index, pl.ds(number, part, stride=heads), :].astype(BF16)
                if offset == 0:
                    rows[head, index, part_of(me), :] = picked
                else:
                    send_buf[head, offset, index] = picked
            if offset:
                input_copy(head, offset).start()
        return carry

    lax.fori_loop(0, here, send_inputs, 0)

    later = lax.broadcasted_iota(jnp.int32, (TILE, TILE), 1)
    earlier = lax.broadcasted_iota(jnp.int32, (TILE, TILE), 0)
    crossed = jnp.bitwise_xor(later, earlier)
    running = jnp.zeros((TILE, TILE), jnp.int32)
    for exponent in range(tile_bits):
        running = running + jnp.where(crossed >= 2**exponent, 1, 0)
    level_ref[...] = jnp.where(earlier <= later, running, -1)
    scaled_t[...] = jnp.zeros_like(scaled_t)
    pulled_t[...] = jnp.zeros_like(pulled_t)

    def near(head):
        for offset in range(1, peers):
            input_copy(head, offset).wait_recv()
        query_t = rows[head, 0].T
        key_t = rows[head, 1].T
        turned[head] = query_t
        state_out[head, 0] = dot(key_t, rows[head, 2]).astype(BF16)
        for degree in range(far):
            level = first_far + degree
            weight = level_factor(level, width) * lw_ref[head, pl.ds(level, 1), :]
            scaled = (query_t.astype(F32) * weight).astype(BF16)
            state_out[head, 1 + degree] = dot(scaled, rows[head, 3]).astype(BF16)
        for offset in range(1, blocks):
            state_copy(head, offset).start()
        for side in range(sides):
            columns = pl.ds(side * SIDE, SIDE)
            depth = pl.ds(0, (side + 1) * SIDE)
            score_t[depth, columns] = dot(
                rows[head, 1, depth, :], query_t[:, side * SIDE : (side + 1) * SIDE]
            )
            pull_t[depth, columns] = dot_nt(rows[head, 2, depth, :], rows[head, 3, columns, :])
        for column in range(tiles):
            columns = pl.ds(column * TILE, TILE)
            sums = {}
            for row in range(column):
                level = (row ^ column).bit_length() + tile_bits
                down = pl.ds(row * TILE, TILE)
                scores = score_t[down, columns]
                pulls = pull_t[down, columns]
                weight = level_factor(level, width) * lw_ref[head, pl.ds(level, 1), columns]
                scaled_t[down, columns] = (weight * scores).astype(BF16)
                pulled_t[down, columns] = (weight * pulls).astype(BF16)
                total = jnp.sum(scores * pulls, axis=0, keepdims=True)
                sums[level] = sums[level] + total if level in sums else total
            scores = score_t[columns, columns]
            pulls = pull_t[columns, columns]
            product = scores * pulls
            levels = level_ref[...]
            weights = jnp.zeros((TILE, TILE), F32)
            for level in range(tile_bits + 1):
                match = levels == level
                weight = level_factor(level, width) * lw_ref[head, pl.ds(level, 1), columns]
                weights = jnp.where(match, weight, weights)
                sums[level] = jnp.sum(jnp.where(match, product, 0.0), axis=0, keepdims=True)
            scaled_t[columns, columns] = (weights * scores).astype(BF16)
            pulled_t[columns, columns] = (weights * pulls).astype(BF16)
            for level in range(local_bits + 1):
                if level in sums:
                    wg_ref[head, pl.ds(level, 1), columns] = (
                        level_factor(level, width) * sums[level]
                    )
                else:
                    wg_ref[head, pl.ds(level, 1), columns] = jnp.zeros((1, TILE), F32)
        for side in range(sides):
            down = pl.ds(side * SIDE, SIDE)
            onward = pl.ds(side * SIDE, toks - side * SIDE)
            depth = (side + 1) * SIDE
            acc[head, 0, down, :] = dot(pulled_t[down, onward], rows[head, 0, onward, :])
            acc[head, 1, down, :] = dot(scaled_t[down, onward], rows[head, 3, onward, :])
            acc_t[head, :, down] = dot(key_t[:, :depth], pulled_t[pl.ds(0, depth), down])

    def finish(head):
        upper = jnp.zeros((width, width), F32)
        lower = [jnp.zeros((width, width), F32) for degree in range(far)]
        for offset in range(1, blocks):
            state_copy(head, offset).wait_recv()
            other = block_from(offset)
            degree_here = degree_of(block, other)
            state = state_in[head, offset].astype(F32)
            upper = upper + jnp.where(other > block, state, 0.0)
            for degree in range(far):
                chosen = jnp.logical_and(other < block, degree_here == degree)
                lower[degree] = lower[degree] + jnp.where(chosen, state, 0.0)
        upper = upper.astype(BF16)
        total_t = acc_t[head]
        wide_t = turned[head].astype(F32)
        for degree in range(far):
            level = first_far + degree
            factor = level_factor(level, width)
            update_t = dot_nt(lower[degree].astype(BF16), rows[head, 3])
            total_t = total_t + (factor * lw_ref[head, pl.ds(level, 1), :]) * update_t
            wg_ref[head, pl.ds(level, 1), :] = factor * jnp.sum(
                wide_t * update_t, axis=0, keepdims=True
            )
        out_rows[head, 0] = total_t.T.astype(BF16)
        out_rows[head, 1] = (acc[head, 0] + dot_nt(rows[head, 2], upper)).astype(BF16)
        out_rows[head, 2] = (acc[head, 1] + dot(rows[head, 1], upper)).astype(BF16)
        for offset in range(1, peers):
            output_copy(head, offset).start()

    def work(step, carry):
        @pl.when(step < here)
        def _():
            near(step)

        @pl.when(step >= 1)
        def _():
            finish(step - 1)

        return carry

    lax.fori_loop(0, here + 1, work, 0)

    def gather(head, carry):
        for offset in range(peers):
            number = source(offset) * here + head
            if offset:
                output_copy(head, offset).wait_recv()
            for index in range(3):
                if offset:
                    piece = land[head, offset, index]
                else:
                    piece = out_rows[head, index, part_of(me), :]
                stage[index, pl.ds(number, part, stride=heads), :] = piece.astype(F32)
        return carry

    lax.fori_loop(0, here, gather, 0)

    for index, ref in enumerate((qo_ref, ko_ref, vo_ref)):
        for start in range(0, part, chunk):
            ref[pl.ds(start, chunk)] = (
                stage[index, pl.ds(start * heads, chunk * heads), :]
                .reshape(chunk, heads, width)
                .astype(BF16)
            )

    def drain(head, carry):
        for offset in range(1, peers):
            input_copy(head, offset).wait_send()
            output_copy(head, offset).wait_send()
        for offset in range(1, blocks):
            state_copy(head, offset).wait_send()
        return carry

    lax.fori_loop(0, here, drain, 0)


def on_device(peers, blocks, queries, keys, values, out_grad, level_weights):
    part, heads, width = queries.shape
    here = heads // peers
    toks = part * peers
    far = blocks.bit_length() - 1
    vmem = pl.BlockSpec(memory_space=pltpu.VMEM)
    narrow = jax.ShapeDtypeStruct(queries.shape, BF16)
    dma = pltpu.SemaphoreType.DMA
    flops = here * (10 * toks * toks * width + 8 * (far + 2) * toks * width * width)
    return pl.pallas_call(
        functools.partial(kernel, peers, blocks),
        out_shape=(narrow, narrow, narrow, jax.ShapeDtypeStruct(level_weights.shape, F32)),
        in_specs=[vmem] * 5,
        out_specs=(vmem,) * 4,
        scratch_shapes=[
            pltpu.VMEM((4, part * heads, width), F32),
            pltpu.VMEM((here, peers, 4, part, width), BF16),
            pltpu.VMEM((here, 4, toks, width), BF16),
            pltpu.VMEM((here, 3, toks, width), BF16),
            pltpu.VMEM((here, peers, 3, part, width), BF16),
            pltpu.VMEM((here, far + 1, width, width), BF16),
            pltpu.VMEM((here, blocks, width, width), BF16),
            pltpu.VMEM((toks, toks), F32),
            pltpu.VMEM((toks, toks), F32),
            pltpu.VMEM((toks, toks), BF16),
            pltpu.VMEM((toks, toks), BF16),
            pltpu.VMEM((TILE, TILE), jnp.int32),
            pltpu.VMEM((here, 2, toks, width), F32),
            pltpu.VMEM((here, width, toks), F32),
            pltpu.VMEM((here, width, toks), BF16),
            dma((here, peers)),
            dma((here, peers)),
            dma((here, peers)),
            dma((here, peers)),
            dma((here, blocks)),
            dma((here, blocks)),
        ],
        compiler_params=pltpu.CompilerParams(
            collective_id=0, has_side_effects=True, vmem_limit_bytes=48 * 2**20
        ),
        cost_estimate=pl.CostEstimate(
            flops=flops, bytes_accessed=7 * part * heads * width * 2, transcendentals=0
        ),
    )(queries, keys, values, out_grad, level_weights)


def solution(mesh):
    wide = P(("seq", "head"), None, None)
    levels = P("head", None, "seq")
    return jax.shard_map(
        functools.partial(on_device, mesh.shape["head"], mesh.shape["seq"]),
        mesh=mesh,
        in_specs=(wide, wide, wide, wide, levels),
        out_specs=(wide, wide, wide, levels),
        check_vma=False,
    )
```

time: 155 us -> 57.2 us (0.37)
  waiting for transfers between devices: 62.9 us -> 0 us
  Pallas kernels: 0 us -> 47.9 us
  starting transfers between devices: 32.2 us -> 0 us
  matrix products: 25.9 us -> 0 us
  local copies, waits for them, and re-layouts: 22.1 us -> 8.17 us
  other arithmetic: 9.34 us -> 0 us
    pallas_call x0 -> x1, Pallas kernels: none -> 47.9 us  [on_device(): pl.pallas_call(functools.partial(kernel, peers, blocks), out_shape=(narro...]
    all_to_all x7 -> x0, waiting for transfers between devices: 44.2 us -> none  [the longest x1 8.1 us: on_device(): lax.all_to_all(key_total.astype(jnp.bfloat16), 'head', split_axis=0, conc...]
    all_to_all x7 -> x0, starting transfers between devices: 27.9 us -> none  [the longest x1 5.17 us: on_device(): lax.all_to_all(queries, 'head', split_axis=1, concat_axis=0, tiled=True)]
    dot_general x10 -> x0, matrix products: 25.9 us -> none  [the longest x1 6.93 us: near_terms(): jnp.einsum('thd,shd->hts', query_rows, key_rows, preferred_element_type=j...]
    ppermute x2 -> x0, waiting for transfers between devices: 18.8 us -> none  [partner(): return lax.ppermute(value, axis, pairs)]
    convert_element_type x5 -> x0, local copies, waits for them, and re-layouts: 6.46 us -> none  [the longest x1 1.55 us: query_states(): jnp.transpose(coefficients, (0, 2, 1))[..., None] * grad_rows[None]]
    and x5 -> x0, other arithmetic: 5.78 us -> none  [near_terms(): matching = (causal & (inside == degree))[None]]
    ppermute x2 -> x0, starting transfers between devices: 4.3 us -> none  [partner(): return lax.ppermute(value, axis, pairs)]
  transfers between devices with their start and end apart: 9 -> 0, of which waited for: 8 -> 0; matrix products, arithmetic and copies ran while one was open for 28% -> 0% of each run, Pallas kernels for 0% -> 0%
where the time goes in v1:
time: 57.2 us; the launch traced here: 56.7 us
  Pallas kernels  47.9 us (84%)
  local copies, waits for them, and re-layouts  8.17 us (14%)
  between operations  0.65 us (1%)
    pallas_call x1, Pallas kernels, on_device(): pl.pallas_call(functools.partial(kernel, peers, blocks), out_shape=(narro...  47.9 us
    unnamed x12, local copies, waits for them, and re-layouts  7.46 us

profile of v1, /device:TPU:0, one launch (start us, length us, event | category | flops | bytes accessed | tf_op | source)
XLA Modules:
  0.0 56.7 jit_solution(16442101480890964585)
XLA Ops:
  0.6 0.9 %copy.9.lw_ref = f32[4,12,512]{2,1,0:T(8,128)S(1)} copy(f32[4,12,512]{2,0,1:T(4,128)} %param.9) | data formatting | bytes 196608 | tf_op args[4]
  1.6 0.0 copy-start
  1.6 1.0 %copy-done = bf16[64,32,128]{2,1,0:T(8,128)(2,1)S(1)} copy-done((bf16[64,32,128]{2,1,0:T(8,128)(2,1)S(1)}, bf16[64,32,128]{2,1,0:T(8,128)(2,1)}, u32[]{:S(2)}) %copy-start) | copy-done | bytes 524312
  2.6 0.0 copy-start.1
  2.6 1.0 %copy-done.1 = bf16[64,32,128]{2,1,0:T(8,128)(2,1)S(1)} copy-done((bf16[64,32,128]{2,1,0:T(8,128)(2,1)S(1)}, bf16[64,32,128]{2,1,0:T(8,128)(2,1)}, u32[]{:S(2)}) %copy-start.1) | copy-done | bytes 524312
  3.6 0.0 copy-start.2
  3.6 1.0 %copy-done.2 = bf16[64,32,128]{2,1,0:T(8,128)(2,1)S(1)} copy-done((bf16[64,32,128]{2,1,0:T(8,128)(2,1)S(1)}, bf16[64,32,128]{2,1,0:T(8,128)(2,1)}, u32[]{:S(2)}) %copy-start.2) | copy-done | bytes 524312
  4.7 0.0 copy-start.3
  4.7 1.0 %copy-done.3 = bf16[64,32,128]{2,1,0:T(8,128)(2,1)S(1)} copy-done((bf16[64,32,128]{2,1,0:T(8,128)(2,1)S(1)}, bf16[64,32,128]{2,1,0:T(8,128)(2,1)}, u32[]{:S(2)}) %copy-start.3) | copy-done | bytes 524312
  5.7 47.9 %shard_map.84 = (bf16[64,32,128]{2,1,0:T(8,128)(2,1)S(1)}, bf16[64,32,128]{2,1,0:T(8,128)(2,1)S(1)}, bf16[64,32,128]{2,1,0:T(8,128)(2,1)S(1)}, f32[4,12,512]{2,1,0:T(8,128)S(1)}) custom-call(bf16[64,32,128]{2,1,0:T(8,128)(2,1)S(1)} %copy-done, bf16[64,32,128]{2,1,0:T(8,128)(2,1)S(1)} %copy-done.1, bf16[64,32,128]{2,1,0:T(8,128)(2,1)S(1)} %copy-done.2, ...), custom_call_target="tpu_custom_call" | custom-call | flops 2415919104 | bytes 3670016 | tf_op jit(solution)/shard_map/pallas_call | solution.py:319
  53.6 0.7 %copy.10 = f32[4,12,512]{2,0,1:T(4,128)} copy(f32[4,12,512]{2,1,0:T(8,128)S(1)} %get-tuple-element.7) | data formatting | bytes 196608 | tf_op jit(solution)/shard_map/pallas_call | solution.py:319
  54.3 0.8 %copy.14 = bf16[64,32,128]{2,1,0:T(8,128)(2,1)} copy(bf16[64,32,128]{2,1,0:T(8,128)(2,1)S(1)} %get-tuple-element.12) | data formatting | bytes 1048576
  55.1 0.8 %copy.15 = bf16[64,32,128]{2,1,0:T(8,128)(2,1)} copy(bf16[64,32,128]{2,1,0:T(8,128)(2,1)S(1)} %get-tuple-element.13) | data formatting | bytes 1048576
  55.9 0.8 %copy.16 = bf16[64,32,128]{2,1,0:T(8,128)(2,1)} copy(bf16[64,32,128]{2,1,0:T(8,128)(2,1)S(1)} %get-tuple-element.14) | data formatting | bytes 1048576
Async XLA Ops:
  1.6 1.0 %copy-start = (bf16[64,32,128]{2,1,0:T(8,128)(2,1)S(1)}, bf16[64,32,128]{2,1,0:T(8,128)(2,1)}, u32[]{:S(2)}) copy-start(bf16[64,32,128]{2,1,0:T(8,128)(2,1)} %q_ref.1) | copy-start | bytes 1572868
  2.6 1.0 %copy-start.1 = (bf16[64,32,128]{2,1,0:T(8,128)(2,1)S(1)}, bf16[64,32,128]{2,1,0:T(8,128)(2,1)}, u32[]{:S(2)}) copy-start(bf16[64,32,128]{2,1,0:T(8,128)(2,1)} %k_ref.1) | copy-start | bytes 1572868
  3.6 1.0 %copy-start.2 = (bf16[64,32,128]{2,1,0:T(8,128)(2,1)S(1)}, bf16[64,32,128]{2,1,0:T(8,128)(2,1)}, u32[]{:S(2)}) copy-start(bf16[64,32,128]{2,1,0:T(8,128)(2,1)} %v_ref.1) | copy-start | bytes 1572868
  4.7 1.0 %copy-start.3 = (bf16[64,32,128]{2,1,0:T(8,128)(2,1)S(1)}, bf16[64,32,128]{2,1,0:T(8,128)(2,1)}, u32[]{:S(2)}) copy-start(bf16[64,32,128]{2,1,0:T(8,128)(2,1)} %g_ref.1) | copy-start | bytes 1572868

commit v2 on v1

--- a/solution.py
+++ b/solution.py
@@ -37,11 +37,15 @@
     k_ref,
     v_ref,
     g_ref,
-    lw_ref,
+    lw_hbm,
     qo_ref,
     ko_ref,
     vo_ref,
     wg_ref,
+    fetched,
+    lw_raw,
+    lw_ref,
+    wg_rows,
     stage,
     send_buf,
     rows,
@@ -63,6 +67,7 @@
     out_recv_sem,
     state_send_sem,
     state_recv_sem,
+    fetch_sem,
 ):
     part, heads, width = q_ref.shape
     here = heads // peers
@@ -98,17 +103,44 @@
             degree = degree + jnp.where(apart, 1, 0)
         return degree
 
+    half = part // 2
+    fetches = []
+    for index, ref in enumerate((k_ref, v_ref, q_ref, g_ref)):
+        index = (1, 2, 0, 3)[index]
+        for piece in range(2):
+            span = pl.ds(piece * half, half)
+            fetches.append(
+                pltpu.make_async_copy(
+                    ref.at[span], fetched.at[index, span], fetch_sem.at[2 * index + piece]
+                )
+            )
+    fetch_levels = pltpu.make_async_copy(lw_hbm, lw_raw, fetch_sem.at[8])
+    for copy in fetches:
+        copy.start()
+    fetch_levels.start()
     barrier = pltpu.get_barrier_semaphore()
     for offset in range(1, peers):
         pl.semaphore_signal(barrier, inc=1, device_id=(block, peer(offset)), device_id_type=MESH)
     for offset in range(1, blocks):
         pl.semaphore_signal(barrier, inc=1, device_id=(block_to(offset), me), device_id_type=MESH)
 
+    later = lax.broadcasted_iota(jnp.int32, (TILE, TILE), 1)
+    earlier = lax.broadcasted_iota(jnp.int32, (TILE, TILE), 0)
+    crossed = jnp.bitwise_xor(later, earlier)
+    running = jnp.zeros((TILE, TILE), jnp.int32)
+    for exponent in range(tile_bits):
+        running = running + jnp.where(crossed >= 2**exponent, 1, 0)
+    level_ref[...] = jnp.where(earlier <= later, running, -1)
+    scaled_t[...] = jnp.zeros_like(scaled_t)
+    pulled_t[...] = jnp.zeros_like(pulled_t)
+
     chunk = 8
-    for index, ref in enumerate((q_ref, k_ref, v_ref, g_ref)):
+    for order, index in enumerate((1, 2, 0, 3)):
         for start in range(0, part, chunk):
+            if start % half == 0:
+                fetches[2 * order + start // half].wait()
             stage[index, pl.ds(start * heads, chunk * heads), :] = (
-                ref[pl.ds(start, chunk)].astype(F32).reshape(chunk * heads, width)
+                fetched[index, pl.ds(start, chunk)].astype(F32).reshape(chunk * heads, width)
             )
 
     pl.semaphore_wait(barrier, peers + blocks - 2)
@@ -159,16 +191,10 @@
         return carry
 
     lax.fori_loop(0, here, send_inputs, 0)
-
-    later = lax.broadcasted_iota(jnp.int32, (TILE, TILE), 1)
-    earlier = lax.broadcasted_iota(jnp.int32, (TILE, TILE), 0)
-    crossed = jnp.bitwise_xor(later, earlier)
-    running = jnp.zeros((TILE, TILE), jnp.int32)
-    for exponent in range(tile_bits):
-        running = running + jnp.where(crossed >= 2**exponent, 1, 0)
-    level_ref[...] = jnp.where(earlier <= later, running, -1)
-    scaled_t[...] = jnp.zeros_like(scaled_t)
-    pulled_t[...] = jnp.zeros_like(pulled_t)
+    fetch_levels.wait()
+    for level in range(first_far + far):
+        for head in range(here):
+            lw_ref[head, pl.ds(level, 1), :] = lw_raw[level, pl.ds(head, 1), :]
 
     def near(head):
         for offset in range(1, peers):
@@ -218,11 +244,11 @@
             pulled_t[columns, columns] = (weights * pulls).astype(BF16)
             for level in range(local_bits + 1):
                 if level in sums:
-                    wg_ref[head, pl.ds(level, 1), columns] = (
+                    wg_rows[head, pl.ds(level, 1), columns] = (
                         level_factor(level, width) * sums[level]
                     )
                 else:
-                    wg_ref[head, pl.ds(level, 1), columns] = jnp.zeros((1, TILE), F32)
+                    wg_rows[head, pl.ds(level, 1), columns] = jnp.zeros((1, TILE), F32)
         for side in range(sides):
             down = pl.ds(side * SIDE, SIDE)
             onward = pl.ds(side * SIDE, toks - side * SIDE)
@@ -251,7 +277,7 @@
             factor = level_factor(level, width)
             update_t = dot_nt(lower[degree].astype(BF16), rows[head, 3])
             total_t = total_t + (factor * lw_ref[head, pl.ds(level, 1), :]) * update_t
-            wg_ref[head, pl.ds(level, 1), :] = factor * jnp.sum(
+            wg_rows[head, pl.ds(level, 1), :] = factor * jnp.sum(
                 wide_t * update_t, axis=0, keepdims=True
             )
         out_rows[head, 0] = total_t.T.astype(BF16)
@@ -272,6 +298,9 @@
         return carry
 
     lax.fori_loop(0, here + 1, work, 0)
+    for level in range(first_far + far):
+        for head in range(here):
+            lw_raw[level, pl.ds(head, 1), :] = wg_rows[head, pl.ds(level, 1), :]
 
     def gather(head, carry):
         for offset in range(peers):
@@ -288,13 +317,25 @@
 
     lax.fori_loop(0, here, gather, 0)
 
+    stores = [pltpu.make_async_copy(lw_raw, wg_ref, fetch_sem.at[8])]
+    stores[0].start()
     for index, ref in enumerate((qo_ref, ko_ref, vo_ref)):
         for start in range(0, part, chunk):
-            ref[pl.ds(start, chunk)] = (
+            fetched[index, pl.ds(start, chunk)] = (
                 stage[index, pl.ds(start * heads, chunk * heads), :]
                 .reshape(chunk, heads, width)
                 .astype(BF16)
             )
+            if (start + chunk) % half == 0:
+                piece = start // half
+                span = pl.ds(piece * half, half)
+                copy = pltpu.make_async_copy(
+                    fetched.at[index, span], ref.at[span], fetch_sem.at[2 * index + piece]
+                )
+                copy.start()
+                stores.append(copy)
+    for copy in stores:
+        copy.wait()
 
     def drain(head, carry):
         for offset in range(1, peers):
@@ -307,21 +348,46 @@
     lax.fori_loop(0, here, drain, 0)
 
 
+def store_kernel(*refs):
+    part = refs[0].shape[0] // 4
+    sem = refs[8]
+    copies = []
+    for index in range(3):
+        for piece in range(4):
+            span = pl.ds(piece * part, part)
+            copies.append(
+                pltpu.make_async_copy(
+                    refs[index].at[span], refs[4 + index].at[span], sem.at[4 * index + piece]
+                )
+            )
+    copies.append(pltpu.make_async_copy(refs[3], refs[7], sem.at[12]))
+    for copy in copies:
+        copy.start()
+    for copy in copies:
+        copy.wait()
+
+
 def on_device(peers, blocks, queries, keys, values, out_grad, level_weights):
     part, heads, width = queries.shape
     here = heads // peers
     toks = part * peers
     far = blocks.bit_length() - 1
-    vmem = pl.BlockSpec(memory_space=pltpu.VMEM)
     narrow = jax.ShapeDtypeStruct(queries.shape, BF16)
     dma = pltpu.SemaphoreType.DMA
     flops = here * (10 * toks * toks * width + 8 * (far + 2) * toks * width * width)
-    return pl.pallas_call(
+    hbm = pl.BlockSpec(memory_space=pltpu.HBM)
+    turned_levels = jnp.transpose(level_weights, (1, 0, 2))
+    shapes = (narrow, narrow, narrow, jax.ShapeDtypeStruct(turned_levels.shape, F32))
+    results = pl.pallas_call(
         functools.partial(kernel, peers, blocks),
-        out_shape=(narrow, narrow, narrow, jax.ShapeDtypeStruct(level_weights.shape, F32)),
-        in_specs=[vmem] * 5,
-        out_specs=(vmem,) * 4,
+        out_shape=shapes,
+        in_specs=[hbm] * 5,
+        out_specs=(hbm,) * 4,
         scratch_shapes=[
+            pltpu.VMEM((4, part, heads, width), BF16),
+            pltpu.VMEM(turned_levels.shape, F32),
+            pltpu.VMEM(level_weights.shape, F32),
+            pltpu.VMEM(level_weights.shape, F32),
             pltpu.VMEM((4, part * heads, width), F32),
             pltpu.VMEM((here, peers, 4, part, width), BF16),
             pltpu.VMEM((here, 4, toks, width), BF16),
@@ -343,14 +409,24 @@
             dma((here, peers)),
             dma((here, blocks)),
             dma((here, blocks)),
+            dma((9,)),
         ],
         compiler_params=pltpu.CompilerParams(
-            collective_id=0, has_side_effects=True, vmem_limit_bytes=48 * 2**20
+            collective_id=0, has_side_effects=True, vmem_limit_bytes=58 * 2**20
         ),
         cost_estimate=pl.CostEstimate(
             flops=flops, bytes_accessed=7 * part * heads * width * 2, transcendentals=0
         ),
-    )(queries, keys, values, out_grad, level_weights)
+    )(queries, keys, values, out_grad, turned_levels)
+    stored = pl.pallas_call(
+        store_kernel,
+        out_shape=shapes,
+        in_specs=[hbm] * 4,
+        out_specs=(hbm,) * 4,
+        scratch_shapes=[dma((13,))],
+        compiler_params=pltpu.CompilerParams(vmem_limit_bytes=58 * 2**20),
+    )(*results)
+    return stored[:3] + (jnp.transpose(stored[3], (1, 0, 2)),)
 
 
 def solution(mesh):

time: 57.2 us -> 102 us (1.78)
  Pallas kernels: 47.9 us -> 101 us
  local copies, waits for them, and re-layouts: 8.17 us -> 0 us
    pallas_call x1 -> x2, Pallas kernels: 47.9 us -> 101 us  [the longest x1 51.8 us: on_device(): pl.pallas_call(store_kernel, out_shape=shapes, in_specs=[hbm] * 4, out_sp...]
    unnamed x12 -> x0, local copies, waits for them, and re-layouts: 7.46 us -> none
where the time goes in v2:
time: 102 us
  Pallas kernels  101 us (99%)
    pallas_call x1, Pallas kernels, on_device(): pl.pallas_call(store_kernel, out_shape=shapes, in_specs=[hbm] * 4, out_sp...  51.8 us
    pallas_call x1, Pallas kernels, on_device(): pl.pallas_call(functools.partial(kernel, peers, blocks), out_shape=shapes...  49.1 us

profile of v2, /device:TPU:0, one launch (start us, length us, event | category | flops | bytes accessed | tf_op | source)
XLA Modules:
  0.0 101.6 jit_solution(16571066154072688456)
XLA Ops:
  0.6 49.1 %shard_map.84 = (bf16[64,32,128]{2,1,0:T(8,128)(2,1)}, bf16[64,32,128]{2,1,0:T(8,128)(2,1)}, bf16[64,32,128]{2,1,0:T(8,128)(2,1)}, f32[12,4,512]{2,1,0:T(4,128)}) custom-call(bf16[64,32,128]{2,1,0:T(8,128)(2,1)} %q_ref.1, bf16[64,32,128]{2,1,0:T(8,128)(2,1)} %k_ref.1, bf16[64,32,128]{2,1,0:T(8,128)(2,1)} %v_ref.1, bf16[64,32,128]{2,1,0:T(8,128)(2,1)} %g_ref.1, ...), custom_call_target="tpu_custom_call" | custom-call | flops 2415919104 | bytes 3670016 | tf_op jit(solution)/shard_map/pallas_call | solution.py:381
  49.7 51.8 %shard_map.85 = (bf16[64,32,128]{2,1,0:T(8,128)(2,1)}, bf16[64,32,128]{2,1,0:T(8,128)(2,1)}, bf16[64,32,128]{2,1,0:T(8,128)(2,1)}, f32[12,4,512]{2,1,0:T(4,128)}) custom-call(bf16[64,32,128]{2,1,0:T(8,128)(2,1)} %get-tuple-element.12.refs_0_, bf16[64,32,128]{2,1,0:T(8,128)(2,1)} %get-tuple-element.13.refs_1_, ...), custom_call_target="tpu_custom_call" | custom-call | tf_op jit(solution)/shard_map/pallas_call | solution.py:421

commit v3 on v2

--- a/solution.py
+++ b/solution.py
@@ -196,9 +196,19 @@
         for head in range(here):
             lw_ref[head, pl.ds(level, 1), :] = lw_raw[level, pl.ds(head, 1), :]
 
+    def send_outputs(head, carry):
+        for offset in range(1, peers):
+            output_copy(head, offset).start()
+        return carry
+
     def near(head):
         for offset in range(1, peers):
             input_copy(head, offset).wait_recv()
+
+        @pl.when(head == here - 1)
+        def _():
+            lax.fori_loop(0, max(here - 2, 0), send_outputs, 0)
+
         query_t = rows[head, 0].T
         key_t = rows[head, 1].T
         turned[head] = query_t
@@ -283,8 +293,10 @@
         out_rows[head, 0] = total_t.T.astype(BF16)
         out_rows[head, 1] = (acc[head, 0] + dot_nt(rows[head, 2], upper)).astype(BF16)
         out_rows[head, 2] = (acc[head, 1] + dot(rows[head, 1], upper)).astype(BF16)
-        for offset in range(1, peers):
-            output_copy(head, offset).start()
+
+        @pl.when(head >= here - 2)
+        def _():
+            send_outputs(head, 0)
 
     def work(step, carry):
         @pl.when(step < here)
@@ -349,21 +361,29 @@
 
 
 def store_kernel(*refs):
-    part = refs[0].shape[0] // 4
-    sem = refs[8]
-    copies = []
+    sources, targets, held, held_levels, sem = refs[:4], refs[4:8], refs[8], refs[9], refs[10]
+    part = held.shape[1] // 2
+    routes = [(sources[3], held_levels, targets[3])]
     for index in range(3):
-        for piece in range(4):
+        for piece in range(2):
             span = pl.ds(piece * part, part)
-            copies.append(
-                pltpu.make_async_copy(
-                    refs[index].at[span], refs[4 + index].at[span], sem.at[4 * index + piece]
-                )
-            )
-    copies.append(pltpu.make_async_copy(refs[3], refs[7], sem.at[12]))
-    for copy in copies:
+            routes.append(
+                (sources[index].at[span], held.at[index, span], targets[index].at[span])
+            )
+    loads = [
+        pltpu.make_async_copy(origin, middle, sem.at[0, number])
+        for number, (origin, middle, target) in enumerate(routes)
+    ]
+    stores = [
+        pltpu.make_async_copy(middle, target, sem.at[1, number])
+        for number, (origin, middle, target) in enumerate(routes)
+    ]
+    for copy in loads:
         copy.start()
-    for copy in copies:
+    for load, store in zip(loads, stores):
+        load.wait()
+        store.start()
+    for copy in stores:
         copy.wait()
 
 
@@ -423,7 +443,11 @@
         out_shape=shapes,
         in_specs=[hbm] * 4,
         out_specs=(hbm,) * 4,
-        scratch_shapes=[dma((13,))],
+        scratch_shapes=[
+            pltpu.VMEM((3, part, heads, width), BF16),
+            pltpu.VMEM(turned_levels.shape, F32),
+            dma((2, 7)),
+        ],
         compiler_params=pltpu.CompilerParams(vmem_limit_bytes=58 * 2**20),
     )(*results)
     return stored[:3] + (jnp.transpose(stored[3], (1, 0, 2)),)

time: 102 us -> 54.5 us (0.53)
  Pallas kernels: 101 us -> 53.4 us
    pallas_call x1, Pallas kernels: 51.8 us -> 2.26 us  [on_device(): pl.pallas_call(store_kernel, out_shape=shapes, in_specs=[hbm] * 4, out_sp...]
    pallas_call x1, Pallas kernels: 49.1 us -> 51.2 us  [on_device(): pl.pallas_call(functools.partial(kernel, peers, blocks), out_shape=shapes...]
where the time goes in v3:
time: 54.5 us; the launch traced here: 54.1 us
  Pallas kernels  53.4 us (98%)
  between operations  0.64 us (1%)
    pallas_call x1, Pallas kernels, on_device(): pl.pallas_call(functools.partial(kernel, peers, blocks), out_shape=shapes...  51.2 us
    pallas_call x1, Pallas kernels, on_device(): pl.pallas_call(store_kernel, out_shape=shapes, in_specs=[hbm] * 4, out_sp...  2.26 us

profile of v3, /device:TPU:0, one launch (start us, length us, event | category | flops | bytes accessed | tf_op | source)
XLA Modules:
  0.0 54.1 jit_solution(5335685251620660451)
XLA Ops:
  0.6 51.2 %shard_map.84 = (bf16[64,32,128]{2,1,0:T(8,128)(2,1)}, bf16[64,32,128]{2,1,0:T(8,128)(2,1)}, bf16[64,32,128]{2,1,0:T(8,128)(2,1)}, f32[12,4,512]{2,1,0:T(4,128)}) custom-call(bf16[64,32,128]{2,1,0:T(8,128)(2,1)} %q_ref.1, bf16[64,32,128]{2,1,0:T(8,128)(2,1)} %k_ref.1, bf16[64,32,128]{2,1,0:T(8,128)(2,1)} %v_ref.1, bf16[64,32,128]{2,1,0:T(8,128)(2,1)} %g_ref.1, ...), custom_call_target="tpu_custom_call" | custom-call | flops 2415919104 | bytes 3670016 | tf_op jit(solution)/shard_map/pallas_call | solution.py:401
  51.8 2.3 %shard_map.85 = (bf16[64,32,128]{2,1,0:T(8,128)(2,1)}, bf16[64,32,128]{2,1,0:T(8,128)(2,1)}, bf16[64,32,128]{2,1,0:T(8,128)(2,1)}, f32[12,4,512]{2,1,0:T(4,128)}) custom-call(bf16[64,32,128]{2,1,0:T(8,128)(2,1)} %get-tuple-element.12.refs_0_, bf16[64,32,128]{2,1,0:T(8,128)(2,1)} %get-tuple-element.13.refs_1_, ...), custom_call_target="tpu_custom_call" | custom-call | tf_op jit(solution)/shard_map/pallas_call | solution.py:441

commit v4 on v3

--- a/solution.py
+++ b/solution.py
@@ -196,22 +196,13 @@
         for head in range(here):
             lw_ref[head, pl.ds(level, 1), :] = lw_raw[level, pl.ds(head, 1), :]
 
-    def send_outputs(head, carry):
-        for offset in range(1, peers):
-            output_copy(head, offset).start()
-        return carry
-
-    def near(head):
+    def states(head):
         for offset in range(1, peers):
             input_copy(head, offset).wait_recv()
-
-        @pl.when(head == here - 1)
-        def _():
-            lax.fori_loop(0, max(here - 2, 0), send_outputs, 0)
-
         query_t = rows[head, 0].T
         key_t = rows[head, 1].T
-        turned[head] = query_t
+        turned[head, 0] = query_t
+        turned[head, 1] = key_t
         state_out[head, 0] = dot(key_t, rows[head, 2]).astype(BF16)
         for degree in range(far):
             level = first_far + degree
@@ -220,11 +211,13 @@
             state_out[head, 1 + degree] = dot(scaled, rows[head, 3]).astype(BF16)
         for offset in range(1, blocks):
             state_copy(head, offset).start()
+
+    def near(head):
         for side in range(sides):
             columns = pl.ds(side * SIDE, SIDE)
             depth = pl.ds(0, (side + 1) * SIDE)
             score_t[depth, columns] = dot(
-                rows[head, 1, depth, :], query_t[:, side * SIDE : (side + 1) * SIDE]
+                rows[head, 1, depth, :], turned[head, 0, :, columns]
             )
             pull_t[depth, columns] = dot_nt(rows[head, 2, depth, :], rows[head, 3, columns, :])
         for column in range(tiles):
@@ -265,7 +258,9 @@
             depth = (side + 1) * SIDE
             acc[head, 0, down, :] = dot(pulled_t[down, onward], rows[head, 0, onward, :])
             acc[head, 1, down, :] = dot(scaled_t[down, onward], rows[head, 3, onward, :])
-            acc_t[head, :, down] = dot(key_t[:, :depth], pulled_t[pl.ds(0, depth), down])
+            acc_t[head, :, down] = dot(
+                turned[head, 1, :, pl.ds(0, depth)], pulled_t[pl.ds(0, depth), down]
+            )
 
     def finish(head):
         upper = jnp.zeros((width, width), F32)
@@ -281,7 +276,7 @@
                 lower[degree] = lower[degree] + jnp.where(chosen, state, 0.0)
         upper = upper.astype(BF16)
         total_t = acc_t[head]
-        wide_t = turned[head].astype(F32)
+        wide_t = turned[head, 0].astype(F32)
         for degree in range(far):
             level = first_far + degree
             factor = level_factor(level, width)
@@ -293,19 +288,21 @@
         out_rows[head, 0] = total_t.T.astype(BF16)
         out_rows[head, 1] = (acc[head, 0] + dot_nt(rows[head, 2], upper)).astype(BF16)
         out_rows[head, 2] = (acc[head, 1] + dot(rows[head, 1], upper)).astype(BF16)
-
-        @pl.when(head >= here - 2)
-        def _():
-            send_outputs(head, 0)
+        for offset in range(1, peers):
+            output_copy(head, offset).start()
 
     def work(step, carry):
         @pl.when(step < here)
         def _():
-            near(step)
+            states(step)
 
         @pl.when(step >= 1)
         def _():
             finish(step - 1)
+
+        @pl.when(step < here)
+        def _():
+            near(step)
 
         return carry
 
@@ -422,7 +419,7 @@
             pltpu.VMEM((TILE, TILE), jnp.int32),
             pltpu.VMEM((here, 2, toks, width), F32),
             pltpu.VMEM((here, width, toks), F32),
-            pltpu.VMEM((here, width, toks), BF16),
+            pltpu.VMEM((here, 2, width, toks), BF16),
             dma((here, peers)),
             dma((here, peers)),
             dma((here, peers)),

time: 54.5 us -> 52.3 us (0.960)
  Pallas kernels: 53.4 us -> 51.3 us
    pallas_call x1, Pallas kernels: 51.2 us -> 49.1 us  [on_device(): pl.pallas_call(functools.partial(kernel, peers, blocks), out_shape=shapes...]
where the time goes in v4:
time: 52.3 us; the launch traced here: 52 us
  Pallas kernels  51.3 us (98%)
  between operations  0.64 us (1%)
    pallas_call x1, Pallas kernels, on_device(): pl.pallas_call(functools.partial(kernel, peers, blocks), out_shape=shapes...  49.1 us
    pallas_call x1, Pallas kernels, on_device(): pl.pallas_call(store_kernel, out_shape=shapes, in_specs=[hbm] * 4, out_sp...  2.26 us

profile of v4, /device:TPU:0, one launch (start us, length us, event | category | flops | bytes accessed | tf_op | source)
XLA Modules:
  0.0 52.0 jit_solution(1773359947913069847)
XLA Ops:
  0.6 49.1 %shard_map.84 = (bf16[64,32,128]{2,1,0:T(8,128)(2,1)}, bf16[64,32,128]{2,1,0:T(8,128)(2,1)}, bf16[64,32,128]{2,1,0:T(8,128)(2,1)}, f32[12,4,512]{2,1,0:T(4,128)}) custom-call(bf16[64,32,128]{2,1,0:T(8,128)(2,1)} %q_ref.1, bf16[64,32,128]{2,1,0:T(8,128)(2,1)} %k_ref.1, bf16[64,32,128]{2,1,0:T(8,128)(2,1)} %v_ref.1, bf16[64,32,128]{2,1,0:T(8,128)(2,1)} %g_ref.1, ...), custom_call_target="tpu_custom_call" | custom-call | flops 2415919104 | bytes 3670016 | tf_op jit(solution)/shard_map/pallas_call | solution.py:398
  49.7 2.3 %shard_map.85 = (bf16[64,32,128]{2,1,0:T(8,128)(2,1)}, bf16[64,32,128]{2,1,0:T(8,128)(2,1)}, bf16[64,32,128]{2,1,0:T(8,128)(2,1)}, f32[12,4,512]{2,1,0:T(4,128)}) custom-call(bf16[64,32,128]{2,1,0:T(8,128)(2,1)} %get-tuple-element.12.refs_0_, bf16[64,32,128]{2,1,0:T(8,128)(2,1)} %get-tuple-element.13.refs_1_, ...), custom_call_target="tpu_custom_call" | custom-call | tf_op jit(solution)/shard_map/pallas_call | solution.py:438
